TPU v7x, 32 devices: a whole 2x2x4 slice. The times are simulated.
32 devices in a mesh: seq: 8 (over y, x, core), dp: 4 (over z).
Axes of the slice: x: 2, y: 2, z: 4, core: 2. Of those that a mesh axis runs over, the one named last changes fastest.
Arguments:
- queries: bfloat16 [4, 4096, 1024], P('dp', 'seq'), may hold values from -6 to 6
- key_rows: bfloat16 [4, 4096, 1024], P('dp', 'seq'), may hold values from -6 to 6
- value_rows: bfloat16 [4, 4096, 1024], P('dp', 'seq'), may hold values from -6 to 6
- gate_rows: bfloat16 [4, 4096, 1024], P('dp', 'seq'), may hold values from -6 to 6
- cotangent: bfloat16 [4, 4096, 1024], P('dp', 'seq'), may hold values from -6 to 6
- far_blocks: int32 [4, 32, 4], P('dp'), may hold values from 0 to 31, as said below
- treated: int32 [4, 32], P('dp'), may hold values 0 or 1
- norm_gain: float32 [1024], replicated, may hold values from 0.1 to 1.9
- out_weight: bfloat16 [1024, 1024], replicated, may hold values from -0.1875 to 0.1875
Outputs:
- output: bfloat16 [4, 4096, 1024], P('dp', 'seq')
- grad_queries: bfloat16 [4, 4096, 1024], P('dp', 'seq')
- grad_keys: bfloat16 [4, 4096, 1024], P('dp', 'seq')
- grad_values: bfloat16 [4, 4096, 1024], P('dp', 'seq')
- grad_gate: bfloat16 [4, 4096, 1024], P('dp', 'seq')
- grad_weight: float32 [1024, 1024], P(('seq', 'dp'))
- grad_gain: float32 [1024], replicated
Inputs may be any that keep to these rules, and one draw needn't show every extreme that they name: `far_blocks`: every entry names a block of the same history that is held by another index of seq than its query block. Of the 16 entries of the query blocks held by index s of seq, 3 name blocks of index (s + o) mod 8 for o = 1 and o = 2, and 2 for each other o from 3 to 7; which entries these are, and which block of that index, are drawn.
All inputs are finite; a program needn't handle non-finite values. No bound on the sum of `treated` on one device may be relied on, other than what follows from the above.
Results may differ from a plain program's by a relative error of at most 0.0065.
Values may be sent and summed in bfloat16 or wider, within the bound.
A program may use at most 192 MiB of HBM per device.

v0:
```python
import jax
import jax.numpy as jnp
from jax import lax
from jax.sharding import PartitionSpec as P

HEADS = 8
HEAD_DIM = 128
BLK = 128
FAR = 4
epsilon = 1e-05


def from_behind(value, axis, by):
    peers = lax.axis_size(axis)
    pairs = [(i, i + by) for i in range(peers) if 0 <= i + by < peers]
    return lax.ppermute(value, axis, pairs)


def to_heads(rows):
    return rows.reshape(rows.shape[:-1] + (HEADS, rows.shape[-1] // HEADS))


def as_bf16(values):
    return values.astype(jnp.bfloat16)


def pair_scores(query_part, key_part):
    scores = jnp.einsum(
        "pqhd,pkhd->phqk",
        to_heads(query_part),
        to_heads(key_part),
        preferred_element_type=jnp.float32,
    )
    return scores * HEAD_DIM ** (-0.5)


def pair_forward(query_part, key_part, value_part, pair_mask):
    weights = as_bf16(jax.nn.silu(pair_scores(query_part, key_part)) * pair_mask[:, None])
    result = jnp.einsum(
        "phqk,pkhd->pqhd", weights, to_heads(value_part), preferred_element_type=jnp.float32
    )
    return result.reshape(query_part.shape)


def pair_backward(query_part, key_part, value_part, grad_part, pair_mask):
    scores = pair_scores(query_part, key_part)
    logistic = jax.nn.sigmoid(scores)
    weights = as_bf16(jax.nn.silu(scores) * pair_mask[:, None])
    grad_heads = to_heads(grad_part)
    grad_weights = jnp.einsum(
        "pqhd,pkhd->phqk", grad_heads, to_heads(value_part), preferred_element_type=jnp.float32
    )
    grad_value = jnp.einsum(
        "phqk,pqhd->pkhd", weights, grad_heads, preferred_element_type=jnp.float32
    )
    grad_scores = as_bf16(
        grad_weights
        * logistic
        * (1.0 + scores * (1.0 - logistic))
        * pair_mask[:, None]
        * HEAD_DIM ** (-0.5)
    )
    grad_query = jnp.einsum(
        "phqk,pkhd->pqhd", grad_scores, to_heads(key_part), preferred_element_type=jnp.float32
    )
    grad_key = jnp.einsum(
        "phqk,pqhd->pkhd", grad_scores, to_heads(query_part), preferred_element_type=jnp.float32
    )
    row_shape = query_part.shape
    return (
        grad_query.reshape(row_shape),
        grad_key.reshape(row_shape),
        grad_value.reshape(row_shape),
    )


def far_plan(far_all, my_index, seq_count, blocks, capacity):
    block_ids = far_all.reshape(seq_count, blocks * FAR)
    owners = block_ids // blocks
    local_ids = block_ids % blocks
    positions = jnp.arange(blocks * FAR)
    same_owner = owners[:, :, None] == owners[:, None, :]
    before = positions[None, :] < positions[:, None]
    slot_rank = jnp.sum(same_owner & before[None], axis=2)
    slot_ids = jnp.arange(capacity)
    send_hit = (owners[:, None, :] == my_index) & (slot_rank[:, None, :] == slot_ids[None, :, None])
    all_local = jnp.sum(jnp.where(send_hit, local_ids[:, None, :], 0), axis=2).reshape(-1)
    all_ok = jnp.any(send_hit, axis=2).reshape(-1)
    my_owners = lax.dynamic_index_in_dim(owners, my_index, 0, keepdims=False)
    my_ranks = lax.dynamic_index_in_dim(slot_rank, my_index, 0, keepdims=False)
    slot_count = seq_count * capacity
    read_at = my_owners * capacity + my_ranks
    back_hit = read_at[None, :] == jnp.arange(slot_count)[:, None]
    return (all_local, all_ok, read_at, back_hit)


def body(
    queries, key_rows, value_rows, gate_rows, cotangent, far_blocks, treated, norm_gain, out_weight
):
    width = queries.shape[2]
    blocks = queries.shape[1] // BLK
    seq_count = lax.axis_size("seq")
    my_index = lax.axis_index("seq")
    requests = blocks * FAR
    capacity = (requests + seq_count - 2) // (seq_count - 1)
    slot_count = seq_count * capacity
    query_blocks = queries[0].reshape(blocks, BLK, width)
    key_blocks = key_rows[0].reshape(blocks, BLK, width)
    value_blocks = value_rows[0].reshape(blocks, BLK, width)
    both_blocks = jnp.concatenate([key_blocks, value_blocks], axis=2)
    from_prev = from_behind(both_blocks[blocks - 1], "seq", 1)
    prev_both = jnp.concatenate([from_prev[None], both_blocks[:-1]], axis=0)
    prev_keys = prev_both[:, :, :width]
    prev_values = prev_both[:, :, width:]
    causal = jnp.tril(jnp.ones((BLK, BLK), jnp.float32))[None]
    all_ones = jnp.ones((1, BLK, BLK), jnp.float32)
    all_local, all_ok, read_at, back_hit = far_plan(
        far_blocks[0], my_index, seq_count, blocks, capacity
    )
    block_ids = lax.dynamic_slice_in_dim(far_blocks[0], my_index * blocks, blocks, 0).reshape(
        requests
    )
    far_mask = treated[0][block_ids].astype(jnp.float32)[:, None, None]
    far_queries = jnp.repeat(query_blocks, FAR, axis=0)
    back_matrix = back_hit.astype(jnp.bfloat16)
    local_onehot = ((all_local[None, :] == jnp.arange(blocks)[:, None]) & all_ok[None, :]).astype(
        jnp.bfloat16
    )
    diag_out = pair_forward(query_blocks, key_blocks, value_blocks, causal)
    prev_out = pair_forward(query_blocks, prev_keys, prev_values, all_ones)
    send_both = jnp.where(
        all_ok[:, None, None], both_blocks[all_local], jnp.zeros((), jnp.bfloat16)
    )
    got_both = lax.all_to_all(
        send_both.reshape(seq_count, capacity, BLK, 2 * width),
        "seq",
        split_axis=0,
        concat_axis=0,
        tiled=True,
    )
    received = got_both.reshape(slot_count, BLK, 2 * width)
    far_both = received[read_at]
    far_keys = far_both[:, :, :width]
    far_values = far_both[:, :, width:]
    far_terms = as_bf16(pair_forward(far_queries, far_keys, far_values, far_mask))
    far_sum = (
        lax.optimization_barrier(far_terms)
        .astype(jnp.float32)
        .reshape(blocks, FAR, BLK, width)
        .sum(axis=1)
    )
    attention = (diag_out + prev_out + far_sum).reshape(blocks * BLK, width)
    centered = attention - jnp.mean(attention, axis=1, keepdims=True)
    inv_std = lax.rsqrt(jnp.mean(centered * centered, axis=1, keepdims=True) + epsilon)
    normed = centered * inv_std
    gate_vals = gate_rows[0].astype(jnp.float32)
    mixed = as_bf16(normed * norm_gain * gate_vals)
    output = jnp.dot(mixed, out_weight, preferred_element_type=jnp.float32).astype(jnp.bfloat16)
    grad_in = cotangent[0]
    grad_mixed = lax.dot_general(
        grad_in, out_weight, (((1,), (1,)), ((), ())), preferred_element_type=jnp.float32
    )
    grad_weight = lax.psum_scatter(
        lax.dot_general(
            mixed, grad_in, (((0,), (0,)), ((), ())), preferred_element_type=jnp.float32
        ),
        ("seq", "dp"),
        scatter_dimension=0,
        tiled=True,
    )
    grad_gate = as_bf16(grad_mixed * normed * norm_gain)
    scaled = grad_mixed * gate_vals
    grad_gain = lax.psum(jnp.sum(scaled * normed, axis=0), ("seq", "dp"))
    grad_hat = scaled * norm_gain
    grad_attn = inv_std * (
        grad_hat
        - jnp.mean(grad_hat, axis=1, keepdims=True)
        - normed * jnp.mean(grad_hat * normed, axis=1, keepdims=True)
    )
    grad_blocks = as_bf16(grad_attn).reshape(blocks, BLK, width)
    dq_diag, dk_diag, dv_diag = pair_backward(
        query_blocks, key_blocks, value_blocks, grad_blocks, causal
    )
    dq_prev, dk_prev, dv_prev = pair_backward(
        query_blocks, prev_keys, prev_values, grad_blocks, all_ones
    )
    prev_terms = lax.optimization_barrier(as_bf16(jnp.concatenate([dk_prev, dv_prev], axis=2)))
    from_next = from_behind(prev_terms[0], "seq", -1)
    next_terms = jnp.concatenate([prev_terms[1:], from_next[None]], axis=0).astype(jnp.float32)
    far_grads = jnp.repeat(grad_blocks, FAR, axis=0)
    dq_far, dk_far, dv_far = pair_backward(far_queries, far_keys, far_values, far_grads, far_mask)
    query_terms = as_bf16(dq_far)
    back_terms = as_bf16(jnp.concatenate([dk_far, dv_far], axis=2))
    send_back = jnp.dot(
        back_matrix, back_terms.reshape(requests, -1), preferred_element_type=jnp.float32
    )
    send_back = as_bf16(send_back).reshape(slot_count, BLK, 2 * width)
    got_back = lax.all_to_all(
        send_back.reshape(seq_count, capacity, BLK, 2 * width),
        "seq",
        split_axis=0,
        concat_axis=0,
        tiled=True,
    )
    owned_terms = got_back.reshape(slot_count, BLK * 2 * width)
    far_query = (
        lax.optimization_barrier(query_terms)
        .astype(jnp.float32)
        .reshape(blocks, FAR, BLK, width)
        .sum(axis=1)
    )
    owned_sum = jnp.dot(
        local_onehot, lax.optimization_barrier(owned_terms), preferred_element_type=jnp.float32
    )
    owned_sum = owned_sum.reshape(blocks, BLK, 2 * width)
    rows = blocks * BLK
    grad_queries = as_bf16(dq_diag + dq_prev + far_query).reshape(1, rows, width)
    key_total = jnp.concatenate([dk_diag, dv_diag], axis=2) + next_terms + owned_sum
    grad_keys = as_bf16(key_total[:, :, :width]).reshape(1, rows, width)
    grad_values = as_bf16(key_total[:, :, width:]).reshape(1, rows, width)
    return (
        output[None],
        grad_queries,
        grad_keys,
        grad_values,
        grad_gate[None],
        grad_weight,
        grad_gain,
    )


def solution(mesh):
    in_specs = (
        P("dp", "seq", None),
        P("dp", "seq", None),
        P("dp", "seq", None),
        P("dp", "seq", None),
        P("dp", "seq", None),
        P("dp", None, None),
        P("dp", None),
        P(),
        P(),
    )
    out_specs = (
        P("dp", "seq", None),
        P("dp", "seq", None),
        P("dp", "seq", None),
        P("dp", "seq", None),
        P("dp", "seq", None),
        P(("seq", "dp"), None),
        P(),
    )
    return jax.shard_map(body, mesh=mesh, in_specs=in_specs, out_specs=out_specs, check_vma=False)
```

profile of v0, /device:TPU:0, one launch (start us, length us, event | category | flops | bytes accessed | tf_op | source)
XLA Modules:
  0.0 594.2 jit_solution(34854243904092478)
XLA Ops:
  9.1 3.1 pad_maximum_fusion.1
  12.2 7.5 %gather_fusion = bf16[24,128,2048]{2,1,0:T(8,128)(2,1)} fusion(bf16[4,128,2048]{2,1,0:T(8,128)(2,1)} %pad_maximum_fusion.1, s32[1024]{0:T(1024)S(1)} %pad_clamp_fusion.2), kind=kCustom, calls=%fused_computation | custom fusion | bytes 25165920 | tf_op jit(solution)/shard_map/gather | solution.py:132
  19.7 10.6 %broadcast_select_fusion = bf16[8,3,128,2048]{3,2,1,0:T(8,128)(2,1)} fusion(bf16[8,3,128,2048]{3,2,1,0:T(8,128)(2,1)} %bitcast.251, pred[8,3]{1,0:T(8,128)(4,1)S(1)} %copy.282), kind=kLoop, calls=%fused_computation.4 | loop fusion | flops 6291456 | bytes 25165848 | tf_op jit(solution)/shard_map/jit(_where)/select_n | solution.py:131
  30.3 5.5 all-to-all-start
  35.8 1.8 fusion.48
  37.6 3.2 collective-permute-start
  45.4 2.8 fusion.29
  48.2 2.2 fusion.45
  50.4 2.6 fusion.36
  53.7 2.5 copy.336
  56.2 2.3 copy.286
  58.4 4.4 fusion.40
  62.8 2.5 pad_maximum_fusion.3
  65.3 2.3 copy.275
  67.6 2.3 copy.274
  69.8 3.1 fusion.75
  73.0 102.6 %all-to-all-done = bf16[8,3,128,2048]{3,2,1,0:T(8,128)(2,1)} async-done(((bf16[8,3,128,2048]{3,2,1,0:T(8,128)(2,1)}), bf16[8,3,128,2048]{3,2,1,0:T(8,128)(2,1)}, u32[]{:S(2)}, u32[]{:S(2)}) %all-to-all-start) | async-done | bytes 12582944 | tf_op jit(solution)/shard_map/all_to_all | solution.py:134
  175.6 9.5 %gather_fusion.1 = bf16[16,128,2048]{2,1,0:T(8,128)(2,1)} fusion(bf16[24,128,2048]{2,1,0:T(8,128)(2,1)} %bitcast.11, s32[1024]{0:T(1024)S(1)} %pad_clamp_fusion.1), kind=kCustom, calls=%fused_computation.1 | custom fusion | bytes 16777280 | tf_op jit(solution)/shard_map/gather | solution.py:142
  185.1 6.1 %fusion.73 = (bf16[16,128,1024]{2,1,0:T(8,128)(2,1)}, bf16[16,128,1024]{2,1,0:T(8,128)(2,1)}) fusion(bf16[16,128,2048]{2,1,0:T(8,128)(2,1)} %gather_fusion.1), kind=kLoop, calls=%fused_computation.143 | loop fusion | bytes 16777216 | tf_op jit(solution)/shard_map/slice | solution.py:143
  191.1 6.4 %copy.285 = bf16[16,128,1024]{1,2,0:T(8,128)(2,1)} copy(bf16[16,128,1024]{2,1,0:T(8,128)(2,1)} %get-tuple-element.18) | data formatting | bytes 8388608 | tf_op jit(solution)/shard_map/slice | solution.py:143
  197.6 6.3 %copy.284 = bf16[16,128,1024]{1,2,0:T(8,128)(2,1)} copy(bf16[16,128,1024]{2,1,0:T(8,128)(2,1)} %get-tuple-element.19) | data formatting | bytes 8388608 | tf_op jit(solution)/shard_map/slice | solution.py:144
  203.8 2.2 broadcast_in_dim.78
  206.3 5.6 fusion.4
  213.9 2.0 convert_reduce_fusion.1
  215.9 3.1 copy.292
  219.0 5.4 fusion.71
  224.6 2.9 copy.280
  227.5 4.6 fusion.31
  235.0 2.3 copy.300
  237.3 2.2 broadcast_in_dim.80
  239.8 5.0 convolution_convert_fusion.1
  244.8 12.7 %fusion.9 = bf16[16,8,128,128]{2,3,1,0:T(8,128)(2,1)} fusion(f32[16,8,128,128]{3,2,1,0:T(8,128)} %get-tuple-element.29, f32[16]{0:T(128)S(1)} %convert_element_type.121, bf16[16,128,8,128]{1,3,2,0:T(8,128)(2,1)} %bitcast.258, bf16[16,128,8,128]{1,3,2,0:T(8,128)(2,1)} %bitcast.261), kind=kOutput, calls=%fused_computation.20 | convolution fusion | flops 562036736 | bytes 20971584 | tf_op jit(solution)/shard_map/pqhd,pkhd->phqk/dot_general | solution.py:50
  257.4 6.7 %copy.315 = bf16[16,128,1024]{2,1,0:T(8,128)(2,1)} copy(bf16[16,128,1024]{1,2,0:T(8,128)(2,1)} %bitcast.263) | data formatting | bytes 8388608 | tf_op jit(solution)/shard_map/reshape | solution.py:73
  264.1 8.4 %convolution_convert_fusion.2 = bf16[16,8,128,128]{2,3,1,0:T(8,128)(2,1)} fusion(bf16[16,8,128,128]{2,3,1,0:T(8,128)(2,1)} %fusion.9, bf16[16,128,8,128]{1,3,2,0:T(8,128)(2,1)} %bitcast.256), kind=kOutput, calls=%fused_computation.26 | convolution fusion | flops 538968064 | bytes 12582912 | tf_op jit(solution)/shard_map/phqk,pqhd->pkhd/dot_general | solution.py:66
  272.5 6.4 %copy.314 = bf16[16,128,1024]{2,1,0:T(8,128)(2,1)} copy(bf16[16,128,1024]{1,2,0:T(8,128)(2,1)} %bitcast.265) | data formatting | bytes 8388608 | tf_op jit(solution)/shard_map/reshape | solution.py:72
  279.0 8.3 %pad_maximum_fusion = bf16[16,128,2048]{2,1,0:T(8,128)(2,1)} fusion(bf16[16,128,1024]{2,1,0:T(8,128)(2,1)} %copy.315, bf16[16,128,1024]{2,1,0:T(8,128)(2,1)} %copy.314), kind=kLoop, calls=%fused_computation.5 | loop fusion | flops 16777216 | bytes 16777216 | tf_op jit(solution)/shard_map/concatenate | solution.py:193
  287.3 11.3 %copy.339 = bf16[2,8,128,2048]{3,1,2,0:T(8,128)(2,1)} copy(bf16[2,8,128,2048]{3,2,1,0:T(8,128)(2,1)} %bitcast.252) | data formatting | bytes 16777216
  298.6 11.4 %convolution_convert_fusion = bf16[24,262144]{1,0:T(8,128)(2,1)} fusion(bf16[16,262144]{1,0:T(8,128)(2,1)} %bitcast.249, s32[16]{0:T(128)S(1)} %bitcast.300), kind=kOutput, calls=%fused_computation.3 | convolution fusion | flops 207618432 | bytes 20971584 | tf_op jit(solution)/shard_map/dot_general | solution.py:194
  309.9 14.7 %copy.340 = bf16[3,8,128,2048]{3,2,1,0:T(8,128)(2,1)} copy(bf16[3,8,128,2048]{3,1,2,0:T(8,128)(2,1)} %bitcast.247) | data formatting | bytes 25165824
  324.6 17.8 %all-to-all-start.1 = ((bf16[8,3,128,2048]{3,2,1,0:T(8,128)(2,1)}), bf16[8,3,128,2048]{3,2,1,0:T(8,128)(2,1)}, u32[]{:S(2)}, u32[]{:S(2)}) async-start(bf16[8,3,128,2048]{3,2,1,0:T(8,128)(2,1)} %bitcast.250), calls=%async_computation.1 | async-start | bytes 25165824 | tf_op jit(solution)/shard_map/all_to_all | solution.py:198
  342.4 2.6 copy.319
  345.0 4.3 fusion.18
  349.3 2.3 copy.320
  351.6 4.9 fusion.34
  357.2 2.5 copy.338
  359.7 2.4 copy.307
  362.1 3.4 fusion.28
  374.8 2.5 copy.299
  377.3 2.7 add.206
  380.1 2.7 slice.56
  382.7 1.9 slice_bitcast_fusion
  386.1 4.7 convolution_convert_fusion.3
  390.8 2.0 convert_reduce_fusion
  392.8 2.9 copy.305
  395.8 147.2 %psum.7 = f32[1024]{0:T(1024)} all-reduce(f32[1024]{0:T(1024)S(1)} %get-tuple-element.7), channel_id=1, replica_groups=mesh['seq'=8,'dp'=4] {'seq','dp'}, use_global_device_ids=true, to_apply=%region_11.12 | all-reduce | flops 1024 | bytes 8192 | tf_op jit(solution)/shard_map/psum | solution.py:173
  543.0 3.1 fusion.76
  548.4 2.2 fusion.30
  550.6 2.2 fusion.69
  552.9 11.7 %copy.341 = bf16[3,8,128,2048]{3,1,2,0:T(8,128)(2,1)S(1)} copy(bf16[3,8,128,2048]{3,2,1,0:T(8,128)(2,1)} %bitcast.95) | data formatting | bytes 25165824
  564.6 3.3 fusion.56
  567.8 4.5 copy.354
  572.3 5.4 copy.316
  577.7 4.6 fusion.11
  583.4 2.3 copy.318
  (117 shorter events, 29.0 us)
Async XLA Ops:
  7.2 43.2 %copy-start = (bf16[1024,1024]{1,0:T(8,128)(2,1)S(1)}, bf16[1024,1024]{1,0:T(8,128)(2,1)}, u32[]{:S(2)}) copy-start(bf16[1024,1024]{1,0:T(8,128)(2,1)} %param.17) | copy-start | bytes 6291460
  9.0 3.2 copy-start.30
  30.3 5.5 copy-start.11
  30.3 145.3 %all-to-all-start = ((bf16[8,3,128,2048]{3,2,1,0:T(8,128)(2,1)}), bf16[8,3,128,2048]{3,2,1,0:T(8,128)(2,1)}, u32[]{:S(2)}, u32[]{:S(2)}) async-start(bf16[8,3,128,2048]{3,2,1,0:T(8,128)(2,1)} %broadcast_select_fusion), calls=%async_computation | async-start | bytes 25165824 | tf_op jit(solution)/shard_map/all_to_all | solution.py:134
  35.8 5.0 copy-start.32
  37.6 25.2 %collective-permute-start = (bf16[128,2048]{1,0:T(8,128)(2,1)}, bf16[128,2048]{1,0:T(8,128)(2,1)}, u32[]{:S(2)}, u32[]{:S(2)}) collective-permute-start(bf16[128,2048]{1,0:T(8,128)(2,1)} %fusion.48), channel_id=1, source_target_pairs={{0,4},{4,8},{8,12},{12,16},{16,20},{20,24},{24,28},{1,5},{5,9},{9,... | collective-permute-start | bytes 1572872 | tf_op jit(solution)/shard_map/ppermute | solution.py:16
  41.0 1.3 copy-start.20
  45.3 2.8 copy-start.14
  48.2 2.2 copy-start.28
  50.4 2.6 copy-start.1
  58.4 4.4 copy-start.19
  203.8 2.5 copy-start.9
  206.0 5.9 copy-start.7
  206.3 5.6 copy-start.10
  212.0 2.0 copy-start.5
  224.6 2.9 copy-start.29
  227.5 4.6 copy-start.4
  227.5 4.6 copy-start.12
  232.1 1.3 copy-start.2
  237.3 2.5 copy-start.6
  239.4 5.3 copy-start.8
  324.6 228.2 %all-to-all-start.1 = ((bf16[8,3,128,2048]{3,2,1,0:T(8,128)(2,1)}), bf16[8,3,128,2048]{3,2,1,0:T(8,128)(2,1)}, u32[]{:S(2)}, u32[]{:S(2)}) async-start(bf16[8,3,128,2048]{3,2,1,0:T(8,128)(2,1)} %bitcast.250), calls=%async_computation.1 | async-start | bytes 25165824 | tf_op jit(solution)/shard_map/all_to_all | solution.py:198
  342.4 244.6 %reduce-scatter.2.cloned.1.call-start = ((), (), s32[]{:S(2)}) async-start(), calls=%async_computation.3 | async-start | bytes 4325376 | tf_op jit(solution)/shard_map/reduce_scatter | solution.py:163
  356.4 0.7 copy-start.31
  365.5 1.6 copy-start.24
  365.5 1.9 copy-start.26
  368.3 2.3 copy-start.22
  368.3 2.6 copy-start.25
  370.9 1.4 copy-start.15
  372.3 1.0 copy-start.21
  372.3 1.6 copy-start.16
  384.6 193.1 %collective-permute-start.1 = (bf16[128,2048]{0,1:T(8,128)(2,1)}, bf16[128,2048]{0,1:T(8,128)(2,1)}, u32[]{:S(2)}, u32[]{:S(2)}) collective-permute-start(bf16[128,2048]{0,1:T(8,128)(2,1)} %slice_bitcast_fusion), channel_id=1, source_target_pairs={{4,0},{8,4},{12,8},{16,12},{20,16},{24,20},{28,24},{5,1},{9,5},{13... | collective-permute-start | bytes 1572872 | tf_op jit(solution)/shard_map/ppermute | solution.py:16
  543.0 3.1 copy-start.17
  543.0 3.1 copy-start.18
  546.1 2.0 copy-start.3
  546.1 2.2 copy-start.13
  548.4 2.3 copy-start.23
  548.4 2.3 copy-start.27
Sparse Core Ops, SparseCore 0:
  356.6 152.8 reduce-scatter.1
where the time goes:
time: 606 us; the launch traced here: 594 us
  local copies, waits for them, and re-layouts  159 us (26%)
  blocking collectives  147 us (24%)
  waiting for transfers between devices  103 us (17%)
  matrix products  89.9 us (15%)
  other arithmetic  52.6 us (9%)
  starting transfers between devices  27.9 us (5%)
  between operations  14.8 us (2%)
    psum x1, blocking collectives, body(): grad_gain = lax.psum(jnp.sum(scaled * normed, axis=0), ('seq', 'dp'))  147 us
    all_to_all x1, waiting for transfers between devices, body(): lax.all_to_all(send_both.reshape(seq_count, capacity, BLK, 2 * width), 's...  103 us
    unnamed x75, local copies, waits for them, and re-layouts  57.6 us
    all_to_all x1, starting transfers between devices, body(): lax.all_to_all(send_back.reshape(seq_count, capacity, BLK, 2 * width), 's...  17.8 us
    dot_general x3, matrix products, pair_backward(): jnp.einsum('pqhd,pkhd->phqk', grad_heads, to_heads(value_part), preferred...  17.5 us
    slice x2, local copies, waits for them, and re-layouts, body(): far_keys = far_both[:, :, :width]  12.5 us
  transfers between devices with their start and end apart: 5, of which 1 were waited for; matrix products, arithmetic and copies ran while one was open for 21% of the time, Pallas kernels for 0%

commit v1 on v0

--- a/solution.py
+++ b/solution.py
@@ -170,7 +170,9 @@
     )
     grad_gate = as_bf16(grad_mixed * normed * norm_gain)
     scaled = grad_mixed * gate_vals
-    grad_gain = lax.psum(jnp.sum(scaled * normed, axis=0), ("seq", "dp"))
+    grad_gain = jnp.sum(scaled * normed, axis=0)
+    for rr in ("dp", "seq"):
+        grad_gain = lax.psum(grad_gain, axis_name=rr)
     grad_hat = scaled * norm_gain
     grad_attn = inv_std * (
         grad_hat

time: 606 us -> 578 us (0.954)
  the two profiles are of different devices: /device:TPU:0 before, /device:TPU:28 now
where the time goes in v1:
time: 578 us; the launch traced here: 566 us
  local copies, waits for them, and re-layouts  159 us (28%)
  waiting for transfers between devices  117 us (20%)
  blocking collectives  117 us (20%)
  matrix products  89.9 us (16%)
  other arithmetic  52.5 us (9%)
  starting transfers between devices  15.5 us (3%)
  between operations  14.8 us (3%)
    ppermute x2, waiting for transfers between devices, from_behind(): return lax.ppermute(value, axis, pairs)  117 us
    psum x2, blocking collectives, body(): grad_gain = lax.psum(grad_gain, axis_name=rr)  117 us
    unnamed x75, local copies, waits for them, and re-layouts  57.7 us
    dot_general x3, matrix products, pair_backward(): jnp.einsum('pqhd,pkhd->phqk', grad_heads, to_heads(value_part), preferred...  17.6 us
    slice x2, local copies, waits for them, and re-layouts, body(): far_keys = far_both[:, :, :width]  12.4 us
    dot_general x3, matrix products, pair_backward(): jnp.einsum('phqk,pqhd->pkhd', grad_scores, to_heads(query_part), preferre...  12 us
  transfers between devices with their start and end apart: 5, of which 1 were waited for; matrix products, arithmetic and copies ran while one was open for 22% of the time, Pallas kernels for 0%

profile of v1, /device:TPU:28, one launch (start us, length us, event | category | flops | bytes accessed | tf_op | source)
XLA Modules:
  0.0 566.2 jit_solution(10489334604977552154)
XLA Ops:
  9.1 3.1 pad_maximum_fusion.1
  12.2 7.5 %gather_fusion = bf16[24,128,2048]{2,1,0:T(8,128)(2,1)} fusion(bf16[4,128,2048]{2,1,0:T(8,128)(2,1)} %pad_maximum_fusion.1, s32[1024]{0:T(1024)S(1)} %pad_clamp_fusion.2), kind=kCustom, calls=%fused_computation | custom fusion | bytes 25165920 | tf_op jit(solution)/shard_map/gather | solution.py:132
  19.7 10.6 %broadcast_select_fusion = bf16[8,3,128,2048]{3,2,1,0:T(8,128)(2,1)} fusion(bf16[8,3,128,2048]{3,2,1,0:T(8,128)(2,1)} %bitcast.251, pred[8,3]{1,0:T(8,128)(4,1)S(1)} %copy.282), kind=kLoop, calls=%fused_computation.4 | loop fusion | flops 6291456 | bytes 25165848 | tf_op jit(solution)/shard_map/jit(_where)/select_n | solution.py:131
  30.3 6.0 %all-to-all-start = ((bf16[8,3,128,2048]{3,2,1,0:T(8,128)(2,1)}), bf16[8,3,128,2048]{3,2,1,0:T(8,128)(2,1)}, u32[]{:S(2)}, u32[]{:S(2)}) async-start(bf16[8,3,128,2048]{3,2,1,0:T(8,128)(2,1)} %broadcast_select_fusion), calls=%async_computation | async-start | bytes 25165824 | tf_op jit(solution)/shard_map/all_to_all | solution.py:134
  38.1 2.0 collective-permute-start
  44.8 2.8 fusion.29
  47.6 2.2 fusion.45
  49.8 2.6 fusion.36
  53.1 2.5 copy.336
  55.6 2.3 copy.286
  57.8 4.4 fusion.40
  62.2 117.4 %collective-permute-done = bf16[128,2048]{1,0:T(8,128)(2,1)} collective-permute-done((bf16[128,2048]{1,0:T(8,128)(2,1)}, bf16[128,2048]{1,0:T(8,128)(2,1)}, u32[]{:S(2)}, u32[]{:S(2)}) %collective-permute-start) | collective-permute-done | bytes 524320 | tf_op jit(solution)/shard_map/ppermute | solution.py:16
  179.6 2.5 pad_maximum_fusion.3
  182.1 2.3 copy.275
  184.3 2.3 copy.274
  186.6 3.1 fusion.75
  189.7 9.5 %gather_fusion.1 = bf16[16,128,2048]{2,1,0:T(8,128)(2,1)} fusion(bf16[24,128,2048]{2,1,0:T(8,128)(2,1)} %bitcast.11, s32[1024]{0:T(1024)S(1)} %pad_clamp_fusion.1), kind=kCustom, calls=%fused_computation.1 | custom fusion | bytes 16777280 | tf_op jit(solution)/shard_map/gather | solution.py:142
  199.2 6.0 %fusion.73 = (bf16[16,128,1024]{2,1,0:T(8,128)(2,1)}, bf16[16,128,1024]{2,1,0:T(8,128)(2,1)}) fusion(bf16[16,128,2048]{2,1,0:T(8,128)(2,1)} %gather_fusion.1), kind=kLoop, calls=%fused_computation.143 | loop fusion | bytes 16777216 | tf_op jit(solution)/shard_map/slice | solution.py:143
  205.2 6.4 %copy.285 = bf16[16,128,1024]{1,2,0:T(8,128)(2,1)} copy(bf16[16,128,1024]{2,1,0:T(8,128)(2,1)} %get-tuple-element.18) | data formatting | bytes 8388608 | tf_op jit(solution)/shard_map/slice | solution.py:143
  211.6 6.3 %copy.284 = bf16[16,128,1024]{1,2,0:T(8,128)(2,1)} copy(bf16[16,128,1024]{2,1,0:T(8,128)(2,1)} %get-tuple-element.19) | data formatting | bytes 8388608 | tf_op jit(solution)/shard_map/slice | solution.py:144
  217.9 2.2 broadcast_in_dim.78
  220.4 5.6 fusion.4
  228.0 2.0 convert_reduce_fusion.1
  229.9 3.1 copy.292
  233.0 5.4 fusion.71
  238.7 2.9 copy.280
  241.6 4.6 fusion.31
  249.0 2.3 copy.300
  251.3 2.2 broadcast_in_dim.80
  253.8 5.0 convolution_convert_fusion.1
  258.8 12.7 %fusion.9 = bf16[16,8,128,128]{2,3,1,0:T(8,128)(2,1)} fusion(f32[16,8,128,128]{3,2,1,0:T(8,128)} %get-tuple-element.29, f32[16]{0:T(128)S(1)} %convert_element_type.121, bf16[16,128,8,128]{1,3,2,0:T(8,128)(2,1)} %bitcast.258, bf16[16,128,8,128]{1,3,2,0:T(8,128)(2,1)} %bitcast.261), kind=kOutput, calls=%fused_computation.20 | convolution fusion | flops 562036736 | bytes 20971584 | tf_op jit(solution)/shard_map/pqhd,pkhd->phqk/dot_general | solution.py:50
  271.5 6.7 %copy.315 = bf16[16,128,1024]{2,1,0:T(8,128)(2,1)} copy(bf16[16,128,1024]{1,2,0:T(8,128)(2,1)} %bitcast.263) | data formatting | bytes 8388608 | tf_op jit(solution)/shard_map/reshape | solution.py:73
  278.1 8.4 %convolution_convert_fusion.2 = bf16[16,8,128,128]{2,3,1,0:T(8,128)(2,1)} fusion(bf16[16,8,128,128]{2,3,1,0:T(8,128)(2,1)} %fusion.9, bf16[16,128,8,128]{1,3,2,0:T(8,128)(2,1)} %bitcast.256), kind=kOutput, calls=%fused_computation.26 | convolution fusion | flops 538968064 | bytes 12582912 | tf_op jit(solution)/shard_map/phqk,pqhd->pkhd/dot_general | solution.py:66
  286.6 6.4 %copy.314 = bf16[16,128,1024]{2,1,0:T(8,128)(2,1)} copy(bf16[16,128,1024]{1,2,0:T(8,128)(2,1)} %bitcast.265) | data formatting | bytes 8388608 | tf_op jit(solution)/shard_map/reshape | solution.py:72
  293.0 8.3 %pad_maximum_fusion = bf16[16,128,2048]{2,1,0:T(8,128)(2,1)} fusion(bf16[16,128,1024]{2,1,0:T(8,128)(2,1)} %copy.315, bf16[16,128,1024]{2,1,0:T(8,128)(2,1)} %copy.314), kind=kLoop, calls=%fused_computation.5 | loop fusion | flops 16777216 | bytes 16777216 | tf_op jit(solution)/shard_map/concatenate | solution.py:195
  301.3 11.3 %copy.339 = bf16[2,8,128,2048]{3,1,2,0:T(8,128)(2,1)} copy(bf16[2,8,128,2048]{3,2,1,0:T(8,128)(2,1)} %bitcast.252) | data formatting | bytes 16777216
  312.5 11.4 %convolution_convert_fusion = bf16[24,262144]{1,0:T(8,128)(2,1)} fusion(bf16[16,262144]{1,0:T(8,128)(2,1)} %bitcast.249, s32[16]{0:T(128)S(1)} %bitcast.300), kind=kOutput, calls=%fused_computation.3 | convolution fusion | flops 207618432 | bytes 20971584 | tf_op jit(solution)/shard_map/dot_general | solution.py:196
  323.9 14.7 %copy.340 = bf16[3,8,128,2048]{3,2,1,0:T(8,128)(2,1)} copy(bf16[3,8,128,2048]{3,1,2,0:T(8,128)(2,1)} %bitcast.247) | data formatting | bytes 25165824
  338.6 5.3 all-to-all-start.1
  343.9 2.6 copy.319
  346.5 4.3 fusion.18
  350.8 2.3 copy.320
  353.1 4.9 fusion.34
  358.7 2.5 copy.338
  361.2 2.4 copy.307
  363.6 3.5 fusion.28
  376.4 2.5 copy.299
  378.9 2.7 add.208
  381.6 2.7 slice.56
  386.2 2.1 collective-permute-start.1
  388.3 4.8 convolution_convert_fusion.3
  393.1 2.0 convert_reduce_fusion
  395.1 2.9 copy.305
  398.0 8.3 %psum.14 = f32[1024]{0:T(1024)S(1)} all-reduce(f32[1024]{0:T(1024)S(1)} %get-tuple-element.7), channel_id=1, replica_groups=mesh['seq'=8,'dp'=4] {'dp'}, use_global_device_ids=true, to_apply=%region_11.12 | all-reduce | flops 1024 | bytes 8192 | tf_op jit(solution)/shard_map/psum | solution.py:175
  406.3 108.8 %psum.15 = f32[1024]{0:T(1024)} all-reduce(f32[1024]{0:T(1024)S(1)} %psum.14), channel_id=1, replica_groups=mesh['seq'=8,'dp'=4] {'seq'}, use_global_device_ids=true, to_apply=%region_12.13 | all-reduce | flops 1024 | bytes 8192 | tf_op jit(solution)/shard_map/psum | solution.py:175
  515.1 3.1 fusion.76
  520.4 2.2 fusion.30
  522.7 2.2 fusion.69
  524.9 11.7 %copy.341 = bf16[3,8,128,2048]{3,1,2,0:T(8,128)(2,1)S(1)} copy(bf16[3,8,128,2048]{3,2,1,0:T(8,128)(2,1)} %bitcast.95) | data formatting | bytes 25165824
  536.6 3.3 fusion.56
  539.9 4.5 copy.354
  544.4 5.3 copy.316
  549.7 4.6 fusion.11
  555.4 2.3 copy.318
  (118 shorter events, 31.1 us)
Async XLA Ops:
  7.2 42.6 %copy-start = (bf16[1024,1024]{1,0:T(8,128)(2,1)S(1)}, bf16[1024,1024]{1,0:T(8,128)(2,1)}, u32[]{:S(2)}) copy-start(bf16[1024,1024]{1,0:T(8,128)(2,1)} %param.17) | copy-start | bytes 6291460
  9.0 3.2 copy-start.30
  30.3 6.0 %copy-start.11 = (bf16[1,512,1024]{2,1,0:T(8,128)(2,1)S(1)}, bf16[1,512,1024]{2,1,0:T(8,128)(2,1)}, u32[]{:S(2)}) copy-start(bf16[1,512,1024]{2,1,0:T(8,128)(2,1)} %param.10) | copy-start | bytes 3145732
  30.3 159.4 %all-to-all-start = ((bf16[8,3,128,2048]{3,2,1,0:T(8,128)(2,1)}), bf16[8,3,128,2048]{3,2,1,0:T(8,128)(2,1)}, u32[]{:S(2)}, u32[]{:S(2)}) async-start(bf16[8,3,128,2048]{3,2,1,0:T(8,128)(2,1)} %broadcast_select_fusion), calls=%async_computation | async-start | bytes 25165824 | tf_op jit(solution)/shard_map/all_to_all | solution.py:134
  36.3 3.9 copy-start.32
  38.1 141.4 %collective-permute-start = (bf16[128,2048]{1,0:T(8,128)(2,1)}, bf16[128,2048]{1,0:T(8,128)(2,1)}, u32[]{:S(2)}, u32[]{:S(2)}) collective-permute-start(bf16[128,2048]{1,0:T(8,128)(2,1)} %fusion.48), channel_id=1, source_target_pairs={{0,4},{4,8},{8,12},{12,16},{16,20},{20,24},{24,28},{1,5},{5,9},{9,... | collective-permute-start | bytes 1572872 | tf_op jit(solution)/shard_map/ppermute | solution.py:16
  40.4 1.3 copy-start.20
  44.7 2.8 copy-start.14
  47.6 2.2 copy-start.28
  49.8 2.6 copy-start.1
  57.8 121.7 %copy-start.19 = (bf16[3,128,2048]{2,1,0:T(8,128)(2,1)S(1)}, bf16[3,128,2048]{2,1,0:T(8,128)(2,1)}, u32[]{:S(2)}) copy-start(bf16[3,128,2048]{2,1,0:T(8,128)(2,1)} %fusion.29) | copy-start | bytes 4718596
  217.9 2.5 copy-start.9
  220.1 5.9 %copy-start.7 = (bf16[4,4,128,1024]{2,3,1,0:T(8,128)(2,1)}, bf16[4,4,128,1024]{2,3,1,0:T(8,128)(2,1)S(1)}, u32[]{:S(2)}) copy-start(bf16[4,4,128,1024]{2,3,1,0:T(8,128)(2,1)S(1)} %broadcast_in_dim.78) | copy-start | bytes 12582916
  220.4 5.6 copy-start.10
  226.0 2.0 copy-start.5
  238.6 2.9 copy-start.29
  241.6 4.6 copy-start.4
  241.6 4.6 copy-start.12
  246.2 1.3 copy-start.2
  251.3 2.5 copy-start.6
  253.5 5.3 copy-start.8
  338.6 186.3 %all-to-all-start.1 = ((bf16[8,3,128,2048]{3,2,1,0:T(8,128)(2,1)}), bf16[8,3,128,2048]{3,2,1,0:T(8,128)(2,1)}, u32[]{:S(2)}, u32[]{:S(2)}) async-start(bf16[8,3,128,2048]{3,2,1,0:T(8,128)(2,1)} %bitcast.250), calls=%async_computation.1 | async-start | bytes 25165824 | tf_op jit(solution)/shard_map/all_to_all | solution.py:200
  343.9 215.1 %reduce-scatter.2.cloned.1.call-start = ((), (), s32[]{:S(2)}) async-start(), calls=%async_computation.3 | async-start | bytes 4325376 | tf_op jit(solution)/shard_map/reduce_scatter | solution.py:163
  357.9 0.7 copy-start.31
  367.1 1.6 copy-start.24
  367.1 1.9 copy-start.26
  369.9 2.4 copy-start.22
  369.9 2.6 copy-start.25
  372.5 1.4 copy-start.15
  373.9 1.0 copy-start.21
  373.9 1.6 copy-start.16
  386.2 163.5 %collective-permute-start.1 = (bf16[128,2048]{0,1:T(8,128)(2,1)}, bf16[128,2048]{0,1:T(8,128)(2,1)}, u32[]{:S(2)}, u32[]{:S(2)}) collective-permute-start(bf16[128,2048]{0,1:T(8,128)(2,1)} %slice_bitcast_fusion), channel_id=1, source_target_pairs={{4,0},{8,4},{12,8},{16,12},{20,16},{24,20},{28,24},{5,1},{9,5},{13... | collective-permute-start | bytes 1572872 | tf_op jit(solution)/shard_map/ppermute | solution.py:16
  515.1 3.1 copy-start.17
  515.1 3.1 copy-start.18
  518.2 2.0 copy-start.3
  518.2 2.2 copy-start.13
  520.4 2.3 copy-start.23
  520.4 2.3 copy-start.27
Sparse Core Ops, SparseCore 0:
  358.1 142.3 reduce-scatter.1
